TPU v7x, 32 devices: a whole 2x2x4 slice. The times are simulated.
32 devices in a mesh: group: 8 (over y, x, core), replica: 4 (over z).
Axes of the slice: x: 2, y: 2, z: 4, core: 2. Of those that a mesh axis runs over, the one named last changes fastest.
Arguments:
- tokens: bfloat16 [4, 1024, 960], P('replica', 'group'), may hold values from -6 to 6
- positions: int32 [4, 1024], P('replica', 'group'), may hold values from 0 to 999, as said below
- gain_attn: bfloat16 [2, 960], P(None, 'group'), may hold values from 0.5 to 1.5
- w_query: bfloat16 [2, 960, 960], P(None, 'group'), may hold values from -0.1875 to 0.1875
- w_key: bfloat16 [2, 960, 320], P(None, 'group'), may hold values from -0.1875 to 0.1875
- w_value: bfloat16 [2, 960, 320], P(None, 'group'), may hold values from -0.1875 to 0.1875
- w_out: bfloat16 [2, 960, 960], P(None, 'group'), may hold values from -0.5 to 0.5
- gain_ffn: bfloat16 [2, 960], P(None, 'group'), may hold values from 0.5 to 1.5
- w_gate: bfloat16 [2, 960, 2560], P(None, 'group'), may hold values from -0.1875 to 0.1875
- w_up: bfloat16 [2, 960, 2560], P(None, 'group'), may hold values from -0.1875 to 0.1875
- w_down: bfloat16 [2, 2560, 960], P(None, 'group'), may hold values from -0.125 to 0.125
- cotangent: bfloat16 [4, 1024, 960], P('replica', 'group'), may hold values from -6 to 6
Outputs:
- activations: float32 [4, 2, 1024, 960], P('replica', None, 'group')
- grad_tokens: float32 [4, 1024, 960], P('replica', 'group')
- grad_gain_attn: float32 [2, 960], P(None, 'group')
- grad_w_query: float32 [2, 960, 960], P(None, 'group')
- grad_w_key: float32 [2, 960, 320], P(None, 'group')
- grad_w_value: float32 [2, 960, 320], P(None, 'group')
- grad_w_out: float32 [2, 960, 960], P(None, 'group')
- grad_gain_ffn: float32 [2, 960], P(None, 'group')
- grad_w_gate: float32 [2, 960, 2560], P(None, 'group')
- grad_w_up: float32 [2, 960, 2560], P(None, 'group')
- grad_w_down: float32 [2, 2560, 960], P(None, 'group')
Inputs may be any that keep to these rules, and one draw needn't show every extreme that they name: In each sequence positions are 0 at a document's first token and rise by one per token inside a document; every document except a sequence's last has 100 to 1000 tokens; the first token of every sequence has position 0.
All inputs are finite; a program needn't handle non-finite values.
Results may differ from a plain program's by a relative error of at most 0.02.
Values may be sent and summed in bfloat16 or wider, within the bound.
A program may use at most 320 MiB of HBM per device.

v0:
```python
import jax
import jax.numpy as jnp
from jax import lax
from jax.sharding import PartitionSpec as P

HEADS = 15
KV_HEADS = 5
HEAD_DIM = 64
LAYERS = 2
epsilon = 1e-05
rope_base = 100000.0


def forward_dot(left, right):
    return jnp.dot(left, right, preferred_element_type=jnp.float32)


def over_rows(left, right):
    return lax.dot_general(
        left, right, (((0,), (0,)), ((), ())), preferred_element_type=jnp.float32
    )


def against(left, right):
    return lax.dot_general(
        left, right, (((1,), (1,)), ((), ())), preferred_element_type=jnp.float32
    )


def rope_tables(token_positions):
    half_dim = HEAD_DIM // 2
    frequency = rope_base ** (-2.0 * jnp.arange(half_dim, dtype=jnp.float32) / HEAD_DIM)
    angles = token_positions.astype(jnp.float32)[:, None] * frequency[None, :]
    return (jnp.cos(angles)[:, None, :], jnp.sin(angles)[:, None, :])


def rotate(vectors, cosine, sine_table):
    half_dim = HEAD_DIM // 2
    leading, trailing = (vectors[..., :half_dim], vectors[..., half_dim:])
    return jnp.concatenate(
        [leading * cosine - trailing * sine_table, trailing * cosine + leading * sine_table],
        axis=-1,
    )


def rotate_back(vectors, cosine, sine_table):
    half_dim = HEAD_DIM // 2
    leading, trailing = (vectors[..., :half_dim], vectors[..., half_dim:])
    return jnp.concatenate(
        [leading * cosine + trailing * sine_table, trailing * cosine - leading * sine_table],
        axis=-1,
    )


def norm_forward(stream):
    inverse = lax.rsqrt(jnp.mean(stream * stream, axis=-1, keepdims=True) + epsilon)
    return (inverse, stream * inverse)


def norm_back(grad_unit, unit_value, inverse):
    return inverse * (
        grad_unit - unit_value * jnp.mean(grad_unit * unit_value, axis=-1, keepdims=True)
    )


def masked_scores(grouped, key_all, allowed):
    scores = (
        jnp.einsum("qkgd,skd->kgqs", grouped, key_all, preferred_element_type=jnp.float32) * 0.125
    )
    return jnp.where(allowed[None, None], scores, -1e30)


def layer_forward(stream, gathered, allowed, cosine, sine_table):
    gain_attn, w_query, w_key, w_value, w_out, gain_ffn, w_gate, w_up, w_down = gathered
    row_count = stream.shape[0]
    inverse_attn, unit_attn = norm_forward(stream)
    normed_attn = (unit_attn * gain_attn.astype(jnp.float32)).astype(jnp.bfloat16)
    queries = rotate(
        forward_dot(normed_attn, w_query).reshape(row_count, HEADS, HEAD_DIM), cosine, sine_table
    ).astype(jnp.bfloat16)
    own_keys = rotate(
        forward_dot(normed_attn, w_key).reshape(row_count, KV_HEADS, HEAD_DIM), cosine, sine_table
    ).astype(jnp.bfloat16)
    own_values = (
        forward_dot(normed_attn, w_value)
        .astype(jnp.bfloat16)
        .reshape(row_count, KV_HEADS, HEAD_DIM)
    )
    key_all, value_all = (
        lax.all_gather(own_keys, "group", axis=0, tiled=True),
        lax.all_gather(own_values, "group", axis=0, tiled=True),
    )
    grouped = queries.reshape(row_count, KV_HEADS, HEADS // KV_HEADS, HEAD_DIM)
    scores = masked_scores(grouped, key_all, allowed)
    row_max = jnp.max(scores, axis=-1, keepdims=True)
    exponent = jnp.exp(scores - row_max)
    row_total = jnp.sum(exponent, axis=-1, keepdims=True)
    weights_low = (exponent / row_total).astype(jnp.bfloat16)
    mixed_heads = jnp.einsum(
        "kgqs,skd->qkgd", weights_low, value_all, preferred_element_type=jnp.float32
    )
    mixed_heads = mixed_heads.reshape(row_count, HEADS * HEAD_DIM).astype(jnp.bfloat16)
    after_attn = stream + forward_dot(mixed_heads, w_out)
    inverse_ffn, unit_ffn = norm_forward(after_attn)
    normed_ffn = (unit_ffn * gain_ffn.astype(jnp.float32)).astype(jnp.bfloat16)
    gate_value = forward_dot(normed_ffn, w_gate)
    up_value = forward_dot(normed_ffn, w_up)
    hidden = (jax.nn.silu(gate_value) * up_value).astype(jnp.bfloat16)
    result = after_attn + forward_dot(hidden, w_down)
    saved = (
        unit_attn,
        inverse_attn,
        normed_attn,
        grouped,
        row_max,
        row_total,
        mixed_heads,
        unit_ffn,
        inverse_ffn,
        normed_ffn,
        gate_value,
        up_value,
        hidden,
    )
    return (result, saved, (own_keys, own_values), (key_all, value_all))


def replica_total(shares):
    (
        share_gain_attn,
        share_query,
        share_key,
        share_value,
        share_out,
        share_gain_ffn,
        share_gate,
        share_up,
        share_down,
    ) = shares
    return lax.psum(
        (
            share_gain_attn,
            share_query,
            share_key,
            share_value,
            share_out,
            share_gain_ffn,
            share_gate,
            share_up,
            share_down,
        ),
        "replica",
    )


def owned_columns(matrix, owner, members):
    width = matrix.shape[1] // members
    return lax.dynamic_slice_in_dim(matrix, owner * width, width, 1)


def layer_backward(grad_result, gathered, saved, key_all, value_all, allowed, cosine, sine_table):
    gain_attn, w_query, w_key, w_value, w_out, gain_ffn, w_gate, w_up, w_down = gathered
    (
        unit_attn,
        inverse_attn,
        normed_attn,
        grouped,
        row_max,
        row_total,
        mixed_heads,
        unit_ffn,
        inverse_ffn,
        normed_ffn,
        gate_value,
        up_value,
        hidden,
    ) = saved
    row_count = grad_result.shape[0]
    branch_low = grad_result.astype(jnp.bfloat16)
    grad_hidden = against(branch_low, w_down)
    sigmoid_gate = jax.nn.sigmoid(gate_value)
    grad_up_low = (grad_hidden * gate_value * sigmoid_gate).astype(jnp.bfloat16)
    grad_gate_low = (
        grad_hidden * up_value * sigmoid_gate * (1.0 + gate_value * (1.0 - sigmoid_gate))
    ).astype(jnp.bfloat16)
    grad_normed_ffn = against(grad_gate_low, w_gate) + against(grad_up_low, w_up)
    grad_gain_ffn = jnp.sum(grad_normed_ffn * unit_ffn, axis=0)
    grad_after = grad_result + norm_back(
        grad_normed_ffn * gain_ffn.astype(jnp.float32), unit_ffn, inverse_ffn
    )
    after_low = grad_after.astype(jnp.bfloat16)
    grad_mixed = (
        against(after_low, w_out)
        .astype(jnp.bfloat16)
        .reshape(row_count, KV_HEADS, HEADS // KV_HEADS, HEAD_DIM)
    )
    scores = masked_scores(grouped, key_all, allowed)
    weights_soft = jnp.exp(scores - row_max) / row_total
    grad_weights = jnp.einsum(
        "qkgd,skd->kgqs", grad_mixed, value_all, preferred_element_type=jnp.float32
    )
    grad_value_all = jnp.einsum(
        "kgqs,qkgd->skd",
        weights_soft.astype(jnp.bfloat16),
        grad_mixed,
        preferred_element_type=jnp.float32,
    )
    grad_scores = (
        weights_soft * (grad_weights - jnp.sum(grad_weights * weights_soft, axis=-1, keepdims=True))
    ).astype(jnp.bfloat16)
    grad_queries = (
        jnp.einsum("kgqs,skd->qkgd", grad_scores, key_all, preferred_element_type=jnp.float32)
        * 0.125
    )
    grad_key_all = (
        jnp.einsum("kgqs,qkgd->skd", grad_scores, grouped, preferred_element_type=jnp.float32)
        * 0.125
    )
    grad_keys, grad_values = (
        lax.psum_scatter(grad_key_all, "group", scatter_dimension=0, tiled=True),
        lax.psum_scatter(grad_value_all, "group", scatter_dimension=0, tiled=True),
    )
    query_back = rotate_back(grad_queries.reshape(row_count, HEADS, HEAD_DIM), cosine, sine_table)
    query_back = query_back.reshape(row_count, HEADS * HEAD_DIM).astype(jnp.bfloat16)
    key_back = (
        rotate_back(grad_keys, cosine, sine_table)
        .reshape(row_count, KV_HEADS * HEAD_DIM)
        .astype(jnp.bfloat16)
    )
    value_back = grad_values.reshape(row_count, KV_HEADS * HEAD_DIM).astype(jnp.bfloat16)
    grad_normed_attn = (
        against(query_back, w_query) + against(key_back, w_key) + against(value_back, w_value)
    )
    grad_gain_attn = jnp.sum(grad_normed_attn * unit_attn, axis=0)
    grad_stream = grad_after + norm_back(
        grad_normed_attn * gain_attn.astype(jnp.float32), unit_attn, inverse_attn
    )
    owner = lax.axis_index("group")
    members = lax.axis_size("group")
    piece_attn = lax.all_gather(normed_attn, "group", axis=0, tiled=True)
    piece_query = lax.all_gather(query_back, "group", axis=0, tiled=True)
    piece_key = lax.all_gather(key_back, "group", axis=0, tiled=True)
    piece_value = lax.all_gather(value_back, "group", axis=0, tiled=True)
    piece_mixed = lax.all_gather(mixed_heads, "group", axis=0, tiled=True)
    piece_after = lax.all_gather(after_low, "group", axis=0, tiled=True)
    piece_ffn = lax.all_gather(normed_ffn, "group", axis=0, tiled=True)
    piece_gate = lax.all_gather(grad_gate_low, "group", axis=0, tiled=True)
    piece_up = lax.all_gather(grad_up_low, "group", axis=0, tiled=True)
    piece_hidden = lax.all_gather(hidden, "group", axis=0, tiled=True)
    piece_branch = lax.all_gather(branch_low, "group", axis=0, tiled=True)
    left_attn = owned_columns(piece_attn, owner, members)
    left_mixed = owned_columns(piece_mixed, owner, members)
    left_ffn = owned_columns(piece_ffn, owner, members)
    left_hidden = owned_columns(piece_hidden, owner, members)
    gain_shares = (
        lax.psum_scatter(grad_gain_attn, "group", scatter_dimension=0, tiled=True),
        lax.psum_scatter(grad_gain_ffn, "group", scatter_dimension=0, tiled=True),
    )
    shares = (
        gain_shares[0],
        over_rows(left_attn, piece_query),
        over_rows(left_attn, piece_key),
        over_rows(left_attn, piece_value),
        over_rows(left_mixed, piece_after),
        gain_shares[1],
        over_rows(left_ffn, piece_gate),
        over_rows(left_ffn, piece_up),
        over_rows(left_hidden, piece_branch),
    )
    return (grad_stream, shares)


def on_device(
    tokens,
    positions,
    gain_attn,
    w_query,
    w_key,
    w_value,
    w_out,
    gain_ffn,
    w_gate,
    w_up,
    w_down,
    cotangent,
):
    row_count = tokens.shape[1]
    length_all = row_count * lax.axis_size("group")
    row_index = lax.axis_index("group") * row_count + jnp.arange(row_count, dtype=jnp.int32)
    token_positions = positions[0]
    key_index = jnp.arange(length_all, dtype=jnp.int32)
    allowed = (key_index[None, :] <= row_index[:, None]) & (
        key_index[None, :] >= (row_index - token_positions)[:, None]
    )
    cosine, sine_table = rope_tables(token_positions)
    stream = tokens[0].astype(jnp.float32)
    saved_all = []
    own_all = []
    full_all = []
    gathered_all = []
    outputs = []
    for layer_index in range(LAYERS):
        gathered = (
            lax.all_gather(gain_attn[layer_index], "group", axis=0, tiled=True),
            lax.all_gather(w_query[layer_index], "group", axis=0, tiled=True),
            lax.all_gather(w_key[layer_index], "group", axis=0, tiled=True),
            lax.all_gather(w_value[layer_index], "group", axis=0, tiled=True),
            lax.all_gather(w_out[layer_index], "group", axis=0, tiled=True),
            lax.all_gather(gain_ffn[layer_index], "group", axis=0, tiled=True),
            lax.all_gather(w_gate[layer_index], "group", axis=0, tiled=True),
            lax.all_gather(w_up[layer_index], "group", axis=0, tiled=True),
            lax.all_gather(w_down[layer_index], "group", axis=0, tiled=True),
        )
        stream, saved, own_pair, full_pair = layer_forward(
            stream, gathered, allowed, cosine, sine_table
        )
        saved_all.append(saved)
        own_all.append(own_pair)
        full_all.append(full_pair)
        gathered_all.append(gathered)
        outputs.append(stream)
    grad_stream = cotangent[0].astype(jnp.float32)
    owned = [None] * LAYERS
    for layer_index in reversed(range(LAYERS)):
        gathered = (
            lax.all_gather(gain_attn[layer_index], "group", axis=0, tiled=True),
            lax.all_gather(w_query[layer_index], "group", axis=0, tiled=True),
            lax.all_gather(w_key[layer_index], "group", axis=0, tiled=True),
            lax.all_gather(w_value[layer_index], "group", axis=0, tiled=True),
            lax.all_gather(w_out[layer_index], "group", axis=0, tiled=True),
            lax.all_gather(gain_ffn[layer_index], "group", axis=0, tiled=True),
            lax.all_gather(w_gate[layer_index], "group", axis=0, tiled=True),
            lax.all_gather(w_up[layer_index], "group", axis=0, tiled=True),
            lax.all_gather(w_down[layer_index], "group", axis=0, tiled=True),
        )
        key_all, value_all = (
            lax.all_gather(own_all[layer_index][0], "group", axis=0, tiled=True),
            lax.all_gather(own_all[layer_index][1], "group", axis=0, tiled=True),
        )
        grad_stream, shares = layer_backward(
            grad_stream,
            gathered,
            saved_all[layer_index],
            key_all,
            value_all,
            allowed,
            cosine,
            sine_table,
        )
        owned[layer_index] = replica_total(shares)
    stacked = tuple(
        (
            jnp.stack([owned[layer_index][member] for layer_index in range(LAYERS)])
            for member in range(9)
        )
    )
    activations = jnp.stack(outputs)[None]
    return (
        activations,
        grad_stream[None],
        stacked[0],
        stacked[1],
        stacked[2],
        stacked[3],
        stacked[4],
        stacked[5],
        stacked[6],
        stacked[7],
        stacked[8],
    )


def solution(mesh):
    in_specs = (
        P("replica", "group", None),
        P("replica", "group"),
        P(None, "group"),
        P(None, "group", None),
        P(None, "group", None),
        P(None, "group", None),
        P(None, "group", None),
        P(None, "group"),
        P(None, "group", None),
        P(None, "group", None),
        P(None, "group", None),
        P("replica", "group", None),
    )
    out_specs = (
        P("replica", None, "group", None),
        P("replica", "group", None),
        P(None, "group"),
        P(None, "group", None),
        P(None, "group", None),
        P(None, "group", None),
        P(None, "group", None),
        P(None, "group"),
        P(None, "group", None),
        P(None, "group", None),
        P(None, "group", None),
    )
    return jax.shard_map(
        on_device, mesh=mesh, in_specs=in_specs, out_specs=out_specs, check_vma=False
    )
```

profile of v0, /device:TPU:0, one launch (start us, length us, event | category | flops | bytes accessed | tf_op | source)
XLA Modules:
  0.0 1593.5 jit_solution(1129092299961670674)
XLA Ops:
  166.6 38.7 %all-gather.90.cloned.1.call-done = bf16[1,2560,960]{2,1,0:T(8,128)(2,1)} async-done(((bf16[1,320,960]{2,1,0:T(8,128)(2,1)}), bf16[1,2560,960]{2,1,0:T(8,128)(2,1)}) %all-gather.90.cloned.1.call-update) | async-done | bytes 4915216 | tf_op jit(solution)/shard_map/all_gather | solution.py:312
  271.7 39.3 %all-gather.98.cloned.1.call-done = bf16[1,960,2560]{2,1,0:T(8,128)(2,1)} async-done(((bf16[1,120,2560]{2,1,0:T(8,128)(2,1)}), bf16[1,960,2560]{2,1,0:T(8,128)(2,1)}) %all-gather.98.cloned.1.call-update) | async-done | bytes 4915216 | tf_op jit(solution)/shard_map/all_gather | solution.py:311
  315.3 39.3 %all-gather.100.cloned.1.call-done = bf16[1,2560,960]{2,1,0:T(8,128)(2,1)} async-done(((bf16[1,320,960]{2,1,0:T(8,128)(2,1)}), bf16[1,2560,960]{2,1,0:T(8,128)(2,1)}) %all-gather.100.cloned.1.call-update) | async-done | bytes 4915216 | tf_op jit(solution)/shard_map/all_gather | solution.py:312
  360.0 36.1 %all-gather.96.cloned.1.call-done = bf16[1,960,2560]{2,1,0:T(8,128)(2,1)} async-done(((bf16[1,120,2560]{2,1,0:T(8,128)(2,1)}), bf16[1,960,2560]{2,1,0:T(8,128)(2,1)}) %all-gather.96.cloned.1.call-update) | async-done | bytes 4915216 | tf_op jit(solution)/shard_map/all_gather | solution.py:310
  446.0 25.5 %reduce-scatter.5.cloned.1.call-done = f32[128,5,64]{0,2,1:T(8,128)} async-done(((f32[1024,5,64]{0,2,1:T(8,128)}), f32[128,5,64]{0,2,1:T(8,128)}) %reduce-scatter.5.cloned.1.call-update) | async-done | bytes 163856 | tf_op jit(solution)/shard_map/reduce_scatter | solution.py:220
  474.8 37.7 %reduce-scatter.7.cloned.1.call-done = f32[128,5,64]{0,2,1:T(8,128)} async-done(((f32[1024,5,64]{0,2,1:T(8,128)}), f32[128,5,64]{0,2,1:T(8,128)}) %reduce-scatter.7.cloned.1.call-update) | async-done | bytes 163856 | tf_op jit(solution)/shard_map/reduce_scatter | solution.py:221
  608.2 25.1 %all-gather.60.cloned.1.call-done = bf16[1024,960]{0,1:T(8,128)(2,1)} async-done(((bf16[128,960]{0,1:T(8,128)(2,1)}), bf16[1024,960]{0,1:T(8,128)(2,1)}) %all-gather.60.cloned.1.call-update) | async-done | bytes 1966096 | tf_op jit(solution)/shard_map/all_gather | solution.py:244
  636.5 37.8 %reduce-scatter.11.cloned.1.call-done = f32[128,5,64]{0,2,1:T(8,128)} async-done(((f32[1024,5,64]{0,2,1:T(8,128)}), f32[128,5,64]{0,2,1:T(8,128)}) %reduce-scatter.11.cloned.1.call-update) | async-done | bytes 163856 | tf_op jit(solution)/shard_map/reduce_scatter | solution.py:221
  675.2 40.1 %reduce-scatter.9.cloned.1.call-done = f32[128,5,64]{0,2,1:T(8,128)} async-done(((f32[1024,5,64]{0,2,1:T(8,128)}), f32[128,5,64]{0,2,1:T(8,128)}) %reduce-scatter.9.cloned.1.call-update) | async-done | bytes 163856 | tf_op jit(solution)/shard_map/reduce_scatter | solution.py:220
  749.0 25.8 %all-gather.50.cloned.1.call-done = bf16[1024,960]{0,1:T(8,128)(2,1)} async-done(((bf16[128,960]{0,1:T(8,128)(2,1)}), bf16[1024,960]{0,1:T(8,128)(2,1)}) %all-gather.50.cloned.1.call-update) | async-done | bytes 1966096 | tf_op jit(solution)/shard_map/all_gather | solution.py:241
  778.0 26.3 %all-gather.56.cloned.1.call-done = bf16[1024,960]{0,1:T(8,128)(2,1)} async-done(((bf16[128,960]{0,1:T(8,128)(2,1)}), bf16[1024,960]{0,1:T(8,128)(2,1)}) %all-gather.56.cloned.1.call-update) | async-done | bytes 1966096 | tf_op jit(solution)/shard_map/all_gather | solution.py:244
  804.3 30.1 %all-gather.58.cloned.1.call-done = bf16[1024,960]{0,1:T(8,128)(2,1)} async-done(((bf16[128,960]{0,1:T(8,128)(2,1)}), bf16[1024,960]{0,1:T(8,128)(2,1)}) %all-gather.58.cloned.1.call-update) | async-done | bytes 1966096 | tf_op jit(solution)/shard_map/all_gather | solution.py:245
  837.7 26.2 %all-gather.78.cloned.1.call-done = bf16[1024,960]{0,1:T(8,128)(2,1)} async-done(((bf16[128,960]{0,1:T(8,128)(2,1)}), bf16[1024,960]{0,1:T(8,128)(2,1)}) %all-gather.78.cloned.1.call-update) | async-done | bytes 1966096 | tf_op jit(solution)/shard_map/all_gather | solution.py:250
  864.0 42.9 %all-gather.76.cloned.1.call-done = bf16[1024,2560]{1,0:T(8,128)(2,1)} async-done(((bf16[128,2560]{1,0:T(8,128)(2,1)}), bf16[1024,2560]{1,0:T(8,128)(2,1)}) %all-gather.76.cloned.1.call-update) | async-done | bytes 5242896 | tf_op jit(solution)/shard_map/all_gather | solution.py:249
  911.2 25.2 %all-gather.102.cloned.1.call-done = bf16[1,1024,960]{1,2,0:T(8,128)(2,1)} async-done(((bf16[1,128,960]{1,2,0:T(8,128)(2,1)}), bf16[1,1024,960]{1,2,0:T(8,128)(2,1)}) %all-gather.102.cloned.1.call-update) | async-done | bytes 1966096 | tf_op jit(solution)/shard_map/all_gather | solution.py:250
  936.4 43.5 %all-gather.80.cloned.1.call-done = bf16[1024,2560]{1,0:T(8,128)(2,1)} async-done(((bf16[128,2560]{1,0:T(8,128)(2,1)}), bf16[1024,2560]{1,0:T(8,128)(2,1)}) %all-gather.80.cloned.1.call-update) | async-done | bytes 5242896 | tf_op jit(solution)/shard_map/all_gather | solution.py:249
  984.2 25.1 %all-gather.68.cloned.1.call-done = bf16[1024,960]{0,1:T(8,128)(2,1)} async-done(((bf16[128,960]{0,1:T(8,128)(2,1)}), bf16[1024,960]{0,1:T(8,128)(2,1)}) %all-gather.68.cloned.1.call-update) | async-done | bytes 1966096 | tf_op jit(solution)/shard_map/all_gather | solution.py:246
  1009.2 43.6 %all-gather.74.cloned.1.call-done = bf16[1024,2560]{1,0:T(8,128)(2,1)} async-done(((bf16[128,2560]{1,0:T(8,128)(2,1)}), bf16[1024,2560]{1,0:T(8,128)(2,1)}) %all-gather.74.cloned.1.call-update) | async-done | bytes 5242896 | tf_op jit(solution)/shard_map/all_gather | solution.py:248
  1057.3 39.1 %all-gather.70.cloned.1.call-done = bf16[1024,2560]{1,0:T(8,128)(2,1)} async-done(((bf16[128,2560]{1,0:T(8,128)(2,1)}), bf16[1024,2560]{1,0:T(8,128)(2,1)}) %all-gather.70.cloned.1.call-update) | async-done | bytes 5242896 | tf_op jit(solution)/shard_map/all_gather | solution.py:247
  1101.0 24.9 %all-gather.64.cloned.1.call-done = bf16[1024,960]{0,1:T(8,128)(2,1)} async-done(((bf16[128,960]{0,1:T(8,128)(2,1)}), bf16[1024,960]{0,1:T(8,128)(2,1)}) %all-gather.64.cloned.1.call-update) | async-done | bytes 1966096 | tf_op jit(solution)/shard_map/all_gather | solution.py:246
  1125.8 43.0 %all-gather.72.cloned.1.call-done = bf16[1024,2560]{1,0:T(8,128)(2,1)} async-done(((bf16[128,2560]{1,0:T(8,128)(2,1)}), bf16[1024,2560]{1,0:T(8,128)(2,1)}) %all-gather.72.cloned.1.call-update) | async-done | bytes 5242896 | tf_op jit(solution)/shard_map/all_gather | solution.py:248
  1173.5 38.4 %all-gather.66.cloned.1.call-done = bf16[1024,2560]{1,0:T(8,128)(2,1)} async-done(((bf16[128,2560]{1,0:T(8,128)(2,1)}), bf16[1024,2560]{1,0:T(8,128)(2,1)}) %all-gather.66.cloned.1.call-update) | async-done | bytes 5242896 | tf_op jit(solution)/shard_map/all_gather | solution.py:247
  1225.3 24.6 %all-reduce.8 = (f32[960]{0:T(1024)S(1)}, f32[960]{0:T(1024)S(1)}, f32[960]{0:T(1024)S(1)}, f32[960]{0:T(1024)S(1)}) all-reduce(f32[960]{0:T(1024)S(1)} %copy-done.74, f32[960]{0:T(1024)S(1)} %get-tuple-element.17, f32[960]{0:T(1024)S(1)} %copy-done.73, f32[960]{0:T(1024)S(1)} %copy-done.75), channel_id=26, replica_groups=mesh['group'=8,'replica'=4] {'group'}, use_global_device_ids=true, to_apply=%region_22.23.clone | all-reduce | flops 3840 | bytes 30720
  1264.0 311.0 %all-reduce.14.cloned.1.call-done = (f32[1,120,960]{2,1,0:T(8,128)}, f32[1,120,960]{2,1,0:T(8,128)}, f32[1,120,320]{1,2,0:T(8,128)}, f32[1,120,320]{1,2,0:T(8,12...) async-done(((f32[1,120,960]{2,1,0:T(8,128)}, ...) | async-done | bytes 9830416 | tf_op jit(solution)/shard_map/psum | solution.py:140
  (421 shorter events, 487.0 us)
Async XLA Ops:
  13.7 191.5 %all-gather.90.cloned.1.call-start = ((), (), s32[]{:S(2)}) async-start(), calls=%async_computation.29 | async-start | bytes 5898240 | tf_op jit(solution)/shard_map/all_gather | solution.py:312
  15.4 223.4 %all-gather.92.cloned.1.call-start = ((), (), s32[]{:S(2)}) async-start(), calls=%async_computation.30 | async-start | bytes 2211840 | tf_op jit(solution)/shard_map/all_gather | solution.py:305
  16.0 252.7 %all-gather.94.cloned.1.call-start = ((), (), s32[]{:S(2)}) async-start(), calls=%async_computation.31 | async-start | bytes 2211840 | tf_op jit(solution)/shard_map/all_gather | solution.py:308
  16.7 294.2 %all-gather.98.cloned.1.call-start = ((), (), s32[]{:S(2)}) async-start(), calls=%async_computation.33 | async-start | bytes 5529600 | tf_op jit(solution)/shard_map/all_gather | solution.py:311
  17.5 337.1 %all-gather.100.cloned.1.call-start = ((), (), s32[]{:S(2)}) async-start(), calls=%async_computation.34 | async-start | bytes 5898240 | tf_op jit(solution)/shard_map/all_gather | solution.py:312
  18.2 377.9 %all-gather.96.cloned.1.call-start = ((), (), s32[]{:S(2)}) async-start(), calls=%async_computation.32 | async-start | bytes 5529600 | tf_op jit(solution)/shard_map/all_gather | solution.py:310
  18.8 452.7 %reduce-scatter.5.cloned.1.call-start = ((), (), s32[]{:S(2)}) async-start(), calls=%async_computation.4 | async-start | bytes 1474560 | tf_op jit(solution)/shard_map/reduce_scatter | solution.py:220
  445.2 188.1 %all-gather.60.cloned.1.call-start = ((), (), s32[]{:S(2)}) async-start(), calls=%async_computation.14 | async-start | bytes 2211840 | tf_op jit(solution)/shard_map/all_gather | solution.py:244
  445.8 228.5 %reduce-scatter.11.cloned.1.call-start = ((), (), s32[]{:S(2)}) async-start(), calls=%async_computation.7 | async-start | bytes 1474560 | tf_op jit(solution)/shard_map/reduce_scatter | solution.py:221
  563.6 181.3 %all-gather.48.cloned.1.call-start = ((), (), s32[]{:S(2)}) async-start(), calls=%async_computation.8 | async-start | bytes 2211840 | tf_op jit(solution)/shard_map/all_gather | solution.py:240
  564.3 210.5 %all-gather.50.cloned.1.call-start = ((), (), s32[]{:S(2)}) async-start(), calls=%async_computation.9 | async-start | bytes 2211840 | tf_op jit(solution)/shard_map/all_gather | solution.py:241
  568.3 236.0 %all-gather.56.cloned.1.call-start = ((), (), s32[]{:S(2)}) async-start(), calls=%async_computation.12 | async-start | bytes 2211840 | tf_op jit(solution)/shard_map/all_gather | solution.py:244
  569.0 265.4 %all-gather.58.cloned.1.call-start = ((), (), s32[]{:S(2)}) async-start(), calls=%async_computation.13 | async-start | bytes 2211840 | tf_op jit(solution)/shard_map/all_gather | solution.py:245
  569.8 294.2 %all-gather.78.cloned.1.call-start = ((), (), s32[]{:S(2)}) async-start(), calls=%async_computation.23 | async-start | bytes 2211840 | tf_op jit(solution)/shard_map/all_gather | solution.py:250
  570.5 336.3 %all-gather.76.cloned.1.call-start = ((), (), s32[]{:S(2)}) async-start(), calls=%async_computation.22 | async-start | bytes 5898240 | tf_op jit(solution)/shard_map/all_gather | solution.py:249
  571.1 365.3 %all-gather.102.cloned.1.call-start = ((), (), s32[]{:S(2)}) async-start(), calls=%async_computation.35 | async-start | bytes 2211840 | tf_op jit(solution)/shard_map/all_gather | solution.py:250
  571.9 408.0 %all-gather.80.cloned.1.call-start = ((), (), s32[]{:S(2)}) async-start(), calls=%async_computation.24 | async-start | bytes 5898240 | tf_op jit(solution)/shard_map/all_gather | solution.py:249
  572.4 436.8 %all-gather.68.cloned.1.call-start = ((), (), s32[]{:S(2)}) async-start(), calls=%async_computation.18 | async-start | bytes 2211840 | tf_op jit(solution)/shard_map/all_gather | solution.py:246
  573.0 479.8 %all-gather.74.cloned.1.call-start = ((), (), s32[]{:S(2)}) async-start(), calls=%async_computation.21 | async-start | bytes 5898240 | tf_op jit(solution)/shard_map/all_gather | solution.py:248
  573.8 522.7 %all-gather.70.cloned.1.call-start = ((), (), s32[]{:S(2)}) async-start(), calls=%async_computation.19 | async-start | bytes 5898240 | tf_op jit(solution)/shard_map/all_gather | solution.py:247
  574.5 551.3 %all-gather.64.cloned.1.call-start = ((), (), s32[]{:S(2)}) async-start(), calls=%async_computation.16 | async-start | bytes 2211840 | tf_op jit(solution)/shard_map/all_gather | solution.py:246
  575.1 593.8 %all-gather.72.cloned.1.call-start = ((), (), s32[]{:S(2)}) async-start(), calls=%async_computation.20 | async-start | bytes 5898240 | tf_op jit(solution)/shard_map/all_gather | solution.py:248
  575.8 636.1 %all-gather.66.cloned.1.call-start = ((), (), s32[]{:S(2)}) async-start(), calls=%async_computation.17 | async-start | bytes 5898240 | tf_op jit(solution)/shard_map/all_gather | solution.py:247
  576.6 998.4 %all-reduce.14.cloned.1.call-start = ((), (), s32[]{:S(2)}) async-start(), calls=%async_computation.36 | async-start | bytes 20316160 | tf_op jit(solution)/shard_map/psum | solution.py:140
  (105 other events, 2377.1 us)
Sparse Core Ops, SparseCore 0:
  10.5 30.1 all-gather.81
  72.4 47.8 all-gather.85
  122.0 39.7 all-gather.87
  164.1 41.1 all-gather.89
  207.5 31.2 all-gather.91
  271.2 39.7 all-gather.97
  313.4 41.1 all-gather.99
  356.3 39.7 all-gather.95
  434.1 37.3 reduce-scatter.4
  475.2 37.3 reduce-scatter.6
  544.4 27.6 all-gather.53
  573.7 30.1 all-gather.61
  636.9 37.3 reduce-scatter.10
  678.0 37.3 reduce-scatter.8
  747.1 27.6 all-gather.49
  776.7 27.6 all-gather.55
  865.7 41.1 all-gather.75
  908.7 27.6 all-gather.101
  938.7 41.1 all-gather.79
  1011.7 41.1 all-gather.73
  1055.3 41.1 all-gather.69
  1127.7 41.1 all-gather.71
  1170.7 41.1 all-gather.65
  1217.5 357.5 all-reduce.13
  (9 shorter events, 247.4 us)
where the time goes:
time: 1600 us; the launch traced here: 1590 us
  waiting for transfers between devices  1100 us (69%)
  blocking collectives  205 us (13%)
  matrix products  191 us (12%)
  other arithmetic  38.1 us (2%)
  local copies, waits for them, and re-layouts  36.4 us (2%)
  between operations  17.4 us (1%)
    psum x1, waiting for transfers between devices, replica_total(): lax.psum((share_gain_attn, share_query, share_key, share_value, share_out...  311 us
    all_gather x2, waiting for transfers between devices, layer_backward(): piece_up = lax.all_gather(grad_up_low, 'group', axis=0, tiled=True)  86.6 us
    all_gather x2, waiting for transfers between devices, layer_backward(): piece_hidden = lax.all_gather(hidden, 'group', axis=0, tiled=True)  86.4 us
    all_gather x2, waiting for transfers between devices, on_device(): lax.all_gather(w_down[layer_index], 'group', axis=0, tiled=True)  78 us
    all_gather x2, waiting for transfers between devices, layer_backward(): piece_gate = lax.all_gather(grad_gate_low, 'group', axis=0, tiled=True)  77.5 us
    reduce_scatter x2, waiting for transfers between devices, layer_backward(): lax.psum_scatter(grad_value_all, 'group', scatter_dimension=0, tiled=True)  75.5 us
    reduce_scatter x2, waiting for transfers between devices, layer_backward(): lax.psum_scatter(grad_key_all, 'group', scatter_dimension=0, tiled=True)  65.6 us
    all_gather x2, waiting for transfers between devices, layer_backward(): piece_branch = lax.all_gather(branch_low, 'group', axis=0, tiled=True)  51.5 us
  transfers between devices with their start and end apart: 33, of which 27 were waited for; matrix products, arithmetic and copies ran while one was open for 13% of the time, Pallas kernels for 0%

commit v1 on v0

--- a/solution.py
+++ b/solution.py
@@ -2,6 +2,7 @@
 import jax.numpy as jnp
 from jax import lax
 from jax.sharding import PartitionSpec as P
+from jax.lax import axis_index, axis_size, ppermute
 
 HEADS = 15
 KV_HEADS = 5
@@ -245,7 +246,22 @@
     piece_after = lax.all_gather(after_low, "group", axis=0, tiled=True)
     piece_ffn = lax.all_gather(normed_ffn, "group", axis=0, tiled=True)
     piece_gate = lax.all_gather(grad_gate_low, "group", axis=0, tiled=True)
-    piece_up = lax.all_gather(grad_up_low, "group", axis=0, tiled=True)
+    made = []
+    total_devices = axis_size("group")
+    for pp in tuple(range(total_devices)):
+        made.append((pp, (pp + 1) % total_devices))
+    arrivals = []
+    for pp in [*range(total_devices)]:
+        arrivals.append((pp, (pp - 1) % total_devices))
+    reached, e_now = ([grad_up_low], [grad_up_low])
+    for _ in range(total_devices // 2):
+        reached.append(ppermute(reached[-1], "group", made))
+    for _ in [*range((total_devices - 1) // 2)]:
+        e_now.append(ppermute(e_now[-1], "group", arrivals))
+    frame_out = jnp.concatenate([*reached[::-1], *e_now[1:]], axis=0)
+    piece_up = jnp.roll(
+        frame_out, (axis_index("group") - total_devices // 2) * grad_up_low.shape[0], axis=0
+    )
     piece_hidden = lax.all_gather(hidden, "group", axis=0, tiled=True)
     piece_branch = lax.all_gather(branch_low, "group", axis=0, tiled=True)
     left_attn = owned_columns(piece_attn, owner, members)

time: 1600 us -> 1540 us (0.963)
  waiting for transfers between devices: 1100 us -> 973 us
  blocking collectives: 205 us -> 238 us
  local copies, waits for them, and re-layouts: 36.4 us -> 60.6 us
  starting transfers between devices: 1.46 us -> 18 us
    all_gather x2 -> x0, waiting for transfers between devices: 86.6 us -> none  [layer_backward(): piece_up = lax.all_gather(grad_up_low, 'group', axis=0, tiled=True)]
    ppermute x0 -> x14, waiting for transfers between devices: none -> 50.2 us  [the longest x8 49.1 us: layer_backward(): reached.append(ppermute(reached[-1], 'group', made))]
    all_gather x2, waiting for transfers between devices: 49.9 us -> 11.3 us  [layer_backward(): piece_ffn = lax.all_gather(normed_ffn, 'group', axis=0, tiled=True)]
    all_gather x2, blocking collectives: 22.6 us -> 54.8 us  [layer_backward(): piece_key = lax.all_gather(key_back, 'group', axis=0, tiled=True)]
    reduce_scatter x2, waiting for transfers between devices: 75.5 us -> 50.2 us  [layer_backward(): lax.psum_scatter(grad_value_all, 'group', scatter_dimension=0, tiled=True)]
    all_gather x2, waiting for transfers between devices: 51.4 us -> 26.3 us  [layer_backward(): piece_mixed = lax.all_gather(mixed_heads, 'group', axis=0, tiled=True)]
    unnamed x207 -> x191, local copies, waits for them, and re-layouts: 12.1 us -> 31.1 us
    ppermute x0 -> x14, starting transfers between devices: none -> 16.3 us  [the longest x6 15.8 us: layer_backward(): e_now.append(ppermute(e_now[-1], 'group', arrivals))]
  transfers between devices with their start and end apart: 33 -> 45, of which waited for: 27 -> 27; matrix products, arithmetic and copies ran while one was open for 13% -> 15% of each run, Pallas kernels for 0% -> 0%
where the time goes in v1:
time: 1540 us; the launch traced here: 1530 us
  waiting for transfers between devices  973 us (63%)
  blocking collectives  238 us (15%)
  matrix products  186 us (12%)
  local copies, waits for them, and re-layouts  60.6 us (4%)
  other arithmetic  38.5 us (2%)
  starting transfers between devices  18 us (1%)
  between operations  17.3 us (1%)
    psum x1, waiting for transfers between devices, replica_total(): lax.psum((share_gain_attn, share_query, share_key, share_value, share_out...  311 us
    all_gather x2, waiting for transfers between devices, layer_backward(): piece_hidden = lax.all_gather(hidden, 'group', axis=0, tiled=True)  86.5 us
    all_gather x2, waiting for transfers between devices, on_device(): lax.all_gather(w_down[layer_index], 'group', axis=0, tiled=True)  78.3 us
    all_gather x2, waiting for transfers between devices, layer_backward(): piece_gate = lax.all_gather(grad_gate_low, 'group', axis=0, tiled=True)  78.2 us
    reduce_scatter x2, waiting for transfers between devices, layer_backward(): lax.psum_scatter(grad_key_all, 'group', scatter_dimension=0, tiled=True)  65.2 us
    all_gather x2, blocking collectives, layer_backward(): piece_key = lax.all_gather(key_back, 'group', axis=0, tiled=True)  54.8 us
    dot_general x14, matrix products, over_rows(): lax.dot_general(left, right, (((0,), (0,)), ((), ())), preferred_element_...  51.6 us
    all_gather x2, waiting for transfers between devices, layer_backward(): piece_branch = lax.all_gather(branch_low, 'group', axis=0, tiled=True)  51.3 us
  transfers between devices with their start and end apart: 45, of which 27 were waited for; matrix products, arithmetic and copies ran while one was open for 15% of the time, Pallas kernels for 0%

profile of v1, /device:TPU:0, one launch (start us, length us, event | category | flops | bytes accessed | tf_op | source)
XLA Modules:
  0.0 1530.3 jit_solution(3843086062338573759)
XLA Ops:
  23.0 15.8 %all-reduce.11 = (bf16[960]{0:T(1024)(128)(2,1)S(1)}, bf16[960]{0:T(1024)(128)(2,1)S(1)}, bf16[960]{0:T(1024)(128)(2,1)S(1)}, bf16[960]{0:T(1024)(128)(2,1)S(1)}) all-reduce(bf16[960]{0:T(1024)(128)(2,1)S(1)} %dynamic-update-slice, bf16[960]{0:T(1024)(128)(2,1)S(1)} %dynamic-update-slice.1, ...), channel_id=2, replica_groups=mesh['group'=8,'replica'=4] {'group'}, use_global_device_ids=true, to_apply=%add | all-reduce | flops 3840 | bytes 15360
  94.8 20.0 %all-gather.11 = bf16[1,960,320]{2,0,1:T(2,128)(2,1)S(1)} all-gather(bf16[1,120,320]{2,0,1:T(2,128)(2,1)S(1)} %copy.82), channel_id=13, replica_groups=mesh['group'=8,'replica'=4] {'group'}, dimensions={1}, use_global_device_ids=true | all-gather | bytes 691200 | tf_op jit(solution)/shard_map/all_gather | solution.py:322
  165.5 39.0 %all-gather.84.cloned.1.call-done = bf16[1,2560,960]{2,1,0:T(8,128)(2,1)} async-done(((bf16[1,320,960]{2,1,0:T(8,128)(2,1)}), bf16[1,2560,960]{2,1,0:T(8,128)(2,1)}) %all-gather.84.cloned.1.call-update) | async-done | bytes 4915216 | tf_op jit(solution)/shard_map/all_gather | solution.py:328
  251.8 15.7 %all-gather.88.cloned.1.call-done = bf16[1,960,960]{2,1,0:T(8,128)(2,1)} async-done(((bf16[1,120,960]{2,1,0:T(8,128)(2,1)}), bf16[1,960,960]{2,1,0:T(8,128)(2,1)}) %all-gather.88.cloned.1.call-update) | async-done | bytes 1843216 | tf_op jit(solution)/shard_map/all_gather | solution.py:324
  270.2 39.5 %all-gather.92.cloned.1.call-done = bf16[1,960,2560]{2,1,0:T(8,128)(2,1)} async-done(((bf16[1,120,2560]{2,1,0:T(8,128)(2,1)}), bf16[1,960,2560]{2,1,0:T(8,128)(2,1)}) %all-gather.92.cloned.1.call-update) | async-done | bytes 4915216 | tf_op jit(solution)/shard_map/all_gather | solution.py:327
  314.1 39.3 %all-gather.94.cloned.1.call-done = bf16[1,2560,960]{2,1,0:T(8,128)(2,1)} async-done(((bf16[1,320,960]{2,1,0:T(8,128)(2,1)}), bf16[1,2560,960]{2,1,0:T(8,128)(2,1)}) %all-gather.94.cloned.1.call-update) | async-done | bytes 4915216 | tf_op jit(solution)/shard_map/all_gather | solution.py:328
  358.8 36.1 %all-gather.90.cloned.1.call-done = bf16[1,960,2560]{2,1,0:T(8,128)(2,1)} async-done(((bf16[1,120,2560]{2,1,0:T(8,128)(2,1)}), bf16[1,960,2560]{2,1,0:T(8,128)(2,1)}) %all-gather.90.cloned.1.call-update) | async-done | bytes 4915216 | tf_op jit(solution)/shard_map/all_gather | solution.py:326
  445.5 25.0 %reduce-scatter.5.cloned.1.call-done = f32[128,5,64]{0,2,1:T(8,128)} async-done(((f32[1024,5,64]{0,2,1:T(8,128)}), f32[128,5,64]{0,2,1:T(8,128)}) %reduce-scatter.5.cloned.1.call-update) | async-done | bytes 163856 | tf_op jit(solution)/shard_map/reduce_scatter | solution.py:221
  472.7 38.8 %reduce-scatter.7.cloned.1.call-done = f32[128,5,64]{0,2,1:T(8,128)} async-done(((f32[1024,5,64]{0,2,1:T(8,128)}), f32[128,5,64]{0,2,1:T(8,128)}) %reduce-scatter.7.cloned.1.call-update) | async-done | bytes 163856 | tf_op jit(solution)/shard_map/reduce_scatter | solution.py:222
  583.3 21.0 %collective-permute-done.8 = bf16[128,2560]{1,0:T(8,128)(2,1)S(1)} collective-permute-done((bf16[128,2560]{1,0:T(8,128)(2,1)S(1)}, bf16[128,2560]{1,0:T(8,128)(2,1)S(1)}, u32[]{:S(2)}, u32[]{:S(2)}) %collective-permute-start.8) | collective-permute-done | bytes 655392 | tf_op jit(solution)/shard_map/ppermute | solution.py:258
  627.8 36.2 %all_gather.175 = bf16[1024,320]{0,1:T(8,128)(2,1)} all-gather(bf16[128,320]{0,1:T(8,128)(2,1)S(1)} %bitcast.438), channel_id=1, replica_groups=mesh['group'=8,'replica'=4] {'group'}, dimensions={0}, use_global_device_ids=true | all-gather | bytes 737280 | tf_op jit(solution)/shard_map/all_gather | solution.py:243
  725.4 40.2 %reduce-scatter.9.cloned.1.call-done = f32[128,5,64]{0,2,1:T(8,128)} async-done(((f32[1024,5,64]{0,2,1:T(8,128)}), f32[128,5,64]{0,2,1:T(8,128)}) %reduce-scatter.9.cloned.1.call-update) | async-done | bytes 163856 | tf_op jit(solution)/shard_map/reduce_scatter | solution.py:221
  766.7 18.6 %all_gather.174 = bf16[1024,320]{0,1:T(8,128)(2,1)} all-gather(bf16[128,320]{0,1:T(8,128)(2,1)S(1)} %bitcast.439), channel_id=1, replica_groups=mesh['group'=8,'replica'=4] {'group'}, dimensions={0}, use_global_device_ids=true | all-gather | bytes 737280 | tf_op jit(solution)/shard_map/all_gather | solution.py:243
  834.7 23.3 %all-gather.48.cloned.1.call-done = bf16[1024,960]{0,1:T(8,128)(2,1)} async-done(((bf16[128,960]{0,1:T(8,128)(2,1)}), bf16[1024,960]{0,1:T(8,128)(2,1)}) %all-gather.48.cloned.1.call-update) | async-done | bytes 1966096 | tf_op jit(solution)/shard_map/all_gather | solution.py:242
  861.3 26.3 %all-gather.54.cloned.1.call-done = bf16[1024,960]{0,1:T(8,128)(2,1)} async-done(((bf16[128,960]{0,1:T(8,128)(2,1)}), bf16[1024,960]{0,1:T(8,128)(2,1)}) %all-gather.54.cloned.1.call-update) | async-done | bytes 1966096 | tf_op jit(solution)/shard_map/all_gather | solution.py:245
  887.5 29.4 %all-gather.56.cloned.1.call-done = bf16[1024,960]{0,1:T(8,128)(2,1)} async-done(((bf16[128,960]{0,1:T(8,128)(2,1)}), bf16[1024,960]{0,1:T(8,128)(2,1)}) %all-gather.56.cloned.1.call-update) | async-done | bytes 1966096 | tf_op jit(solution)/shard_map/all_gather | solution.py:246
  920.2 26.3 %all-gather.72.cloned.1.call-done = bf16[1024,960]{0,1:T(8,128)(2,1)} async-done(((bf16[128,960]{0,1:T(8,128)(2,1)}), bf16[1024,960]{0,1:T(8,128)(2,1)}) %all-gather.72.cloned.1.call-update) | async-done | bytes 1966096 | tf_op jit(solution)/shard_map/all_gather | solution.py:266
  946.5 42.9 %all-gather.70.cloned.1.call-done = bf16[1024,2560]{1,0:T(8,128)(2,1)} async-done(((bf16[128,2560]{1,0:T(8,128)(2,1)}), bf16[1024,2560]{1,0:T(8,128)(2,1)}) %all-gather.70.cloned.1.call-update) | async-done | bytes 5242896 | tf_op jit(solution)/shard_map/all_gather | solution.py:265
  993.7 25.1 %all-gather.96.cloned.1.call-done = bf16[1,1024,960]{1,2,0:T(8,128)(2,1)} async-done(((bf16[1,128,960]{1,2,0:T(8,128)(2,1)}), bf16[1,1024,960]{1,2,0:T(8,128)(2,1)}) %all-gather.96.cloned.1.call-update) | async-done | bytes 1966096 | tf_op jit(solution)/shard_map/all_gather | solution.py:266
  1018.7 43.6 %all-gather.74.cloned.1.call-done = bf16[1024,2560]{1,0:T(8,128)(2,1)} async-done(((bf16[128,2560]{1,0:T(8,128)(2,1)}), bf16[1024,2560]{1,0:T(8,128)(2,1)}) %all-gather.74.cloned.1.call-update) | async-done | bytes 5242896 | tf_op jit(solution)/shard_map/all_gather | solution.py:265
  1066.6 39.3 %all-gather.68.cloned.1.call-done = bf16[1024,2560]{1,0:T(8,128)(2,1)} async-done(((bf16[128,2560]{1,0:T(8,128)(2,1)}), bf16[1024,2560]{1,0:T(8,128)(2,1)}) %all-gather.68.cloned.1.call-update) | async-done | bytes 5242896 | tf_op jit(solution)/shard_map/all_gather | solution.py:248
  1110.5 38.9 %all-gather.64.cloned.1.call-done = bf16[1024,2560]{1,0:T(8,128)(2,1)} async-done(((bf16[128,2560]{1,0:T(8,128)(2,1)}), bf16[1024,2560]{1,0:T(8,128)(2,1)}) %all-gather.64.cloned.1.call-update) | async-done | bytes 5242896 | tf_op jit(solution)/shard_map/all_gather | solution.py:248
  1162.3 24.9 %all-reduce.8 = (f32[960]{0:T(1024)S(1)}, f32[960]{0:T(1024)S(1)}, f32[960]{0:T(1024)S(1)}, f32[960]{0:T(1024)S(1)}) all-reduce(f32[960]{0:T(1024)S(1)} %copy-done.64, f32[960]{0:T(1024)S(1)} %get-tuple-element.18, f32[960]{0:T(1024)S(1)} %copy-done.63, ...), channel_id=26, replica_groups=mesh['group'=8,'replica'=4] {'group'}, use_global_device_ids=true, to_apply=%region_22.23.clone | all-reduce | flops 3840 | bytes 30720
  1201.3 311.5 %all-reduce.14.cloned.1.call-done = (f32[1,120,960]{2,1,0:T(8,128)}, f32[1,120,960]{2,1,0:T(8,128)}, f32[1,120,320]{1,2,0:T(8,128)}, f32[1,120,320]{1,2,0:T(8,12...) async-done(((f32[1,120,960]{2,1,0:T(8,128)}, ...) | async-done | bytes 9830416 | tf_op jit(solution)/shard_map/psum | solution.py:141
  (430 shorter events, 496.4 us)
Async XLA Ops:
  18.0 249.5 %all-gather.88.cloned.1.call-start = ((), (), s32[]{:S(2)}) async-start(), calls=%async_computation.29 | async-start | bytes 2211840 | tf_op jit(solution)/shard_map/all_gather | solution.py:324
  18.7 291.0 %all-gather.92.cloned.1.call-start = ((), (), s32[]{:S(2)}) async-start(), calls=%async_computation.31 | async-start | bytes 5529600 | tf_op jit(solution)/shard_map/all_gather | solution.py:327
  19.5 333.9 %all-gather.94.cloned.1.call-start = ((), (), s32[]{:S(2)}) async-start(), calls=%async_computation.32 | async-start | bytes 5898240 | tf_op jit(solution)/shard_map/all_gather | solution.py:328
  20.2 374.7 %all-gather.90.cloned.1.call-start = ((), (), s32[]{:S(2)}) async-start(), calls=%async_computation.30 | async-start | bytes 5529600 | tf_op jit(solution)/shard_map/all_gather | solution.py:326
  20.8 449.8 %reduce-scatter.5.cloned.1.call-start = ((), (), s32[]{:S(2)}) async-start(), calls=%async_computation.4 | async-start | bytes 1474560 | tf_op jit(solution)/shard_map/reduce_scatter | solution.py:221
  438.8 257.3 %all-gather.50.cloned.1.call-start = ((), (), s32[]{:S(2)}) async-start(), calls=%async_computation.10 | async-start | bytes 2211840 | tf_op jit(solution)/shard_map/all_gather | solution.py:241
  439.6 258.7 %all-gather.52.cloned.1.call-start = ((), (), s32[]{:S(2)}) async-start(), calls=%async_computation.11 | async-start | bytes 2211840 | tf_op jit(solution)/shard_map/all_gather | solution.py:242
  443.7 257.8 %all-gather.60.cloned.1.call-start = ((), (), s32[]{:S(2)}) async-start(), calls=%async_computation.15 | async-start | bytes 2211840 | tf_op jit(solution)/shard_map/all_gather | solution.py:246
  444.3 257.2 %all-gather.58.cloned.1.call-start = ((), (), s32[]{:S(2)}) async-start(), calls=%async_computation.14 | async-start | bytes 2211840 | tf_op jit(solution)/shard_map/all_gather | solution.py:245
  444.9 261.9 %all-gather.66.cloned.1.call-start = ((), (), s32[]{:S(2)}) async-start(), calls=%async_computation.18 | async-start | bytes 2211840 | tf_op jit(solution)/shard_map/all_gather | solution.py:247
  445.5 278.9 %reduce-scatter.11.cloned.1.call-start = ((), (), s32[]{:S(2)}) async-start(), calls=%async_computation.7 | async-start | bytes 1474560 | tf_op jit(solution)/shard_map/reduce_scatter | solution.py:222
  539.8 225.9 %reduce-scatter.9.cloned.1.call-start = ((), (), s32[]{:S(2)}) async-start(), calls=%async_computation.6 | async-start | bytes 1474560 | tf_op jit(solution)/shard_map/reduce_scatter | solution.py:221
  559.5 238.6 %all-gather.46.cloned.1.call-start = ((), (), s32[]{:S(2)}) async-start(), calls=%async_computation.8 | async-start | bytes 2211840 | tf_op jit(solution)/shard_map/all_gather | solution.py:241
  560.1 268.4 %all-gather.62.cloned.1.call-start = ((), (), s32[]{:S(2)}) async-start(), calls=%async_computation.16 | async-start | bytes 2211840 | tf_op jit(solution)/shard_map/all_gather | solution.py:247
  560.8 297.2 %all-gather.48.cloned.1.call-start = ((), (), s32[]{:S(2)}) async-start(), calls=%async_computation.9 | async-start | bytes 2211840 | tf_op jit(solution)/shard_map/all_gather | solution.py:242
  564.9 322.6 %all-gather.54.cloned.1.call-start = ((), (), s32[]{:S(2)}) async-start(), calls=%async_computation.12 | async-start | bytes 2211840 | tf_op jit(solution)/shard_map/all_gather | solution.py:245
  565.7 351.2 %all-gather.56.cloned.1.call-start = ((), (), s32[]{:S(2)}) async-start(), calls=%async_computation.13 | async-start | bytes 2211840 | tf_op jit(solution)/shard_map/all_gather | solution.py:246
  566.3 380.2 %all-gather.72.cloned.1.call-start = ((), (), s32[]{:S(2)}) async-start(), calls=%async_computation.21 | async-start | bytes 2211840 | tf_op jit(solution)/shard_map/all_gather | solution.py:266
  567.0 422.3 %all-gather.70.cloned.1.call-start = ((), (), s32[]{:S(2)}) async-start(), calls=%async_computation.20 | async-start | bytes 5898240 | tf_op jit(solution)/shard_map/all_gather | solution.py:265
  567.6 451.1 %all-gather.96.cloned.1.call-start = ((), (), s32[]{:S(2)}) async-start(), calls=%async_computation.33 | async-start | bytes 2211840 | tf_op jit(solution)/shard_map/all_gather | solution.py:266
  568.2 494.2 %all-gather.74.cloned.1.call-start = ((), (), s32[]{:S(2)}) async-start(), calls=%async_computation.22 | async-start | bytes 5898240 | tf_op jit(solution)/shard_map/all_gather | solution.py:265
  568.9 537.0 %all-gather.68.cloned.1.call-start = ((), (), s32[]{:S(2)}) async-start(), calls=%async_computation.19 | async-start | bytes 5898240 | tf_op jit(solution)/shard_map/all_gather | solution.py:248
  569.7 579.7 %all-gather.64.cloned.1.call-start = ((), (), s32[]{:S(2)}) async-start(), calls=%async_computation.17 | async-start | bytes 5898240 | tf_op jit(solution)/shard_map/all_gather | solution.py:248
  627.7 885.0 %all-reduce.14.cloned.1.call-start = ((), (), s32[]{:S(2)}) async-start(), calls=%async_computation.34 | async-start | bytes 20316160 | tf_op jit(solution)/shard_map/psum | solution.py:141
  (102 other events, 3148.4 us)
Sparse Core Ops, SparseCore 0:
  10.5 30.2 all-gather.75
  72.5 46.5 all-gather.79
  121.3 39.7 all-gather.81
  163.4 41.1 all-gather.83
  206.9 30.7 all-gather.85
  270.0 39.7 all-gather.91
  312.2 41.1 all-gather.93
  355.1 39.7 all-gather.89
  433.2 37.3 reduce-scatter.4
  474.2 37.3 reduce-scatter.6
  543.4 27.8 all-gather.51
  573.0 34.0 all-gather.59
  608.8 36.4 all-gather.57
  647.5 31.3 all-gather.65
  682.6 41.8 reduce-scatter.10
  728.3 37.3 reduce-scatter.8
  767.3 30.6 all-gather.45
  800.0 28.4 all-gather.61
  948.2 41.1 all-gather.69
  991.1 27.6 all-gather.95
  1021.2 41.1 all-gather.73
  1064.8 41.1 all-gather.67
  1108.2 41.1 all-gather.63
  1155.1 357.5 all-reduce.13
  (7 shorter events, 192.4 us)
